TPU v7x, 32 devices: a whole 2x2x4 slice. The times are simulated.
32 devices in a mesh: gx: 2 (over core), ha: 16 (over z, y, x).
Axes of the slice: x: 2, y: 2, z: 4, core: 2. Of those that a mesh axis runs over, the one named last changes fastest.
Arguments:
- level_set: float32 [48, 160, 256], P('ha', 'gx'), may hold values from -6 to 6
- step_length: float32 [1], replicated, may hold values from 0.12 to 0.2
Outputs:
- level_next: float32 [48, 160, 256], P('ha', 'gx')
All inputs are finite; a program needn't handle non-finite values.
Results may differ from a plain program's by a relative error of at most 0.00002.
Values sent between devices are 32-bit elements; how exact they have to be, the bound alone decides.
A program may use at most 64 MiB of HBM per device.

v0:
```python
import jax
import jax.numpy as jnp
from jax import lax
from jax.sharding import PartitionSpec as P

epsilon_weno = 1e-06
speed_rate = 1.0
turn_rate = 1.0


def extended_2(cells, sides, width, closed):
    for axis, dim in sides:
        count = lax.axis_size(axis)
        ends = count if closed else count - 1
        head = lax.slice_in_dim(cells, 0, width, axis=dim)
        tail = lax.slice_in_dim(cells, cells.shape[dim] - width, cells.shape[dim], axis=dim)
        cells = jnp.concatenate(
            [
                lax.ppermute(tail, axis, [(i, (i + 1) % count) for i in range(ends)]),
                cells,
                lax.ppermute(head, axis, [((i + 1) % count, i) for i in range(ends)]),
            ],
            axis=dim,
        )
    return cells


def weno_blend(slope_one, slope_two, slope_three, slope_four, slope_five):
    guess_one = slope_one / 3.0 - 7.0 * slope_two / 6.0 + 11.0 * slope_three / 6.0
    guess_two = -slope_two / 6.0 + 5.0 * slope_three / 6.0 + slope_four / 3.0
    guess_three = slope_three / 3.0 + 5.0 * slope_four / 6.0 - slope_five / 6.0
    smooth_one = (
        13.0 / 12.0 * (slope_one - 2.0 * slope_two + slope_three) ** 2
        + 0.25 * (slope_one - 4.0 * slope_two + 3.0 * slope_three) ** 2
    )
    smooth_two = (
        13.0 / 12.0 * (slope_two - 2.0 * slope_three + slope_four) ** 2
        + 0.25 * (slope_two - slope_four) ** 2
    )
    smooth_three = (
        13.0 / 12.0 * (slope_three - 2.0 * slope_four + slope_five) ** 2
        + 0.25 * (3.0 * slope_three - 4.0 * slope_four + slope_five) ** 2
    )
    weight_one = 0.1 / (smooth_one + epsilon_weno) ** 2
    weight_two = 0.6 / (smooth_two + epsilon_weno) ** 2
    weight_three = 0.3 / (smooth_three + epsilon_weno) ** 2
    weight_sum = weight_one + weight_two + weight_three
    return (
        weight_one * guess_one + weight_two * guess_two + weight_three * guess_three
    ) / weight_sum


def one_sided(padded, axis, count):
    forward_diff = lax.slice_in_dim(padded, 1, count + 6, axis=axis) - lax.slice_in_dim(
        padded, 0, count + 5, axis=axis
    )
    pieces = [
        lax.slice_in_dim(forward_diff, offset, offset + count, axis=axis) for offset in range(6)
    ]
    minus_side = weno_blend(pieces[0], pieces[1], pieces[2], pieces[3], pieces[4])
    plus_side = weno_blend(pieces[5], pieces[4], pieces[3], pieces[2], pieces[1])
    return (minus_side, plus_side)


def combine_rate(minus_x, plus_x, minus_h, plus_h, minus_y, plus_y, cosine_table, sine_table):
    cos_grid = cosine_table[None, :, None]
    sin_grid = sine_table[None, :, None]
    hamilton = speed_rate * (
        cos_grid * (minus_x + plus_x) * 0.5 + sin_grid * (minus_y + plus_y) * 0.5
    ) - turn_rate * jnp.abs((minus_h + plus_h) * 0.5)
    damping = 0.5 * (
        speed_rate * jnp.abs(cos_grid) * (plus_x - minus_x)
        + speed_rate * jnp.abs(sin_grid) * (plus_y - minus_y)
        + turn_rate * (plus_h - minus_h)
    )
    return damping - jnp.maximum(0.0, -hamilton)


def split_rate(widened, headed, block, cosine_table, sine_table):
    minus_x, plus_x = one_sided(widened, 0, block.shape[0])
    minus_h, plus_h = one_sided(headed, 1, block.shape[1])
    minus_y, plus_y = one_sided(pad_sides(block), 2, block.shape[2])
    return combine_rate(minus_x, plus_x, minus_h, plus_h, minus_y, plus_y, cosine_table, sine_table)


def heading_tables(rows_h):
    total_h = lax.axis_size("gx") * rows_h
    global_h = lax.axis_index("gx") * rows_h + jnp.arange(rows_h, dtype=jnp.int32)
    heading = 2.0 * jnp.pi * global_h.astype(jnp.float32) / total_h
    return (jnp.cos(heading), jnp.sin(heading))


def pad_sides(extended):
    return jnp.pad(extended, ((0, 0), (0, 0), (3, 3)))


def on_device(level_set, step_length):
    step_size = step_length[0]
    rows_h = level_set.shape[1]
    cosine_table, sine_table = heading_tables(rows_h)

    def section_rate(section_field):
        widened = extended_2(section_field, (("ha", 0),), 3, False)
        headed = extended_2(section_field, (("gx", 1),), 3, True)
        return split_rate(widened, headed, section_field, cosine_table, sine_table)

    section_one = level_set + step_size * section_rate(level_set)
    section_two = 0.75 * level_set + 0.25 * (section_one + step_size * section_rate(section_one))
    return level_set / 3.0 + 2.0 / 3.0 * (section_two + step_size * section_rate(section_two))


def solution(mesh):
    return jax.shard_map(
        on_device,
        mesh=mesh,
        in_specs=(P("ha", "gx", None), P()),
        out_specs=P("ha", "gx", None),
        check_vma=False,
    )
```

profile of v0, /device:TPU:29, one launch (start us, length us, event | category | flops | bytes accessed | tf_op | source)
XLA Modules:
  0.0 58.9 jit_solution(12027674987049393923)
XLA Ops:
  0.0 3.1 %collective-permute-start = (f32[3,80,256]{2,1,0:T(8,128)}, f32[3,80,256]{2,1,0:T(8,128)S(1)}, u32[]{:S(2)}, u32[]{:S(2)}) collective-permute-start(f32[3,80,256]{2,1,0:T(8,128)} %param.2), channel_id=1, source_target_pairs={{0,1},{1,2},{2,3},{3,4},{4,5},{5,6},{6,7},{7,8},{8,9},{9,10},{10,1... | collective-permute-start | bytes 737288 | tf_op jit(solution)/shard_map/ppermute | solution.py:19
  3.1 3.1 %collective-permute-start.1 = (f32[3,80,256]{2,1,0:T(8,128)}, f32[3,80,256]{2,1,0:T(8,128)S(1)}, u32[]{:S(2)}, u32[]{:S(2)}) collective-permute-start(f32[3,80,256]{2,1,0:T(8,128)} %param.2), channel_id=1, source_target_pairs={{1,0},{2,1},{3,2},{4,3},{5,4},{6,5},{7,6},{8,7},{9,8},{10,9},{11,1... | collective-permute-start | bytes 737288 | tf_op jit(solution)/shard_map/ppermute | solution.py:21
  6.2 0.8 %fusion.9 = (f32[3,3,256]{2,1,0:T(4,128)S(1)}, f32[3,3,256]{2,1,0:T(4,128)S(1)}) fusion(f32[3,80,256]{2,1,0:T(8,128)} %param.2), kind=kLoop, calls=%fused_computation.33 | loop fusion | bytes 36864 | tf_op jit(solution)/shard_map/slice | solution.py:16
  7.0 1.2 %collective-permute-start.2 = (f32[3,3,256]{2,1,0:T(4,128)S(1)}, f32[3,3,256]{2,1,0:T(4,128)S(1)}, u32[]{:S(2)}, u32[]{:S(2)}) collective-permute-start(f32[3,3,256]{2,1,0:T(4,128)S(1)} %get-tuple-element.9), channel_id=1, source_target_pairs={{0,16},{16,0},{1,17},{17,1},{2,18},{18,2},{3,19},{19,3},{4,20},{20... | collective-permute-start | bytes 27656 | tf_op jit(solution)/shard_map/ppermute | solution.py:19
  8.2 0.1 collective-permute-start.3
  8.3 0.0 copy-start
  8.3 1.4 %fusion = f32[3,80,261]{2,1,0:T(8,128)S(1)} fusion(f32[3,80,256]{2,1,0:T(8,128)} %param.2), kind=kLoop, calls=%fused_computation.11 | loop fusion | flops 62640 | bytes 496320 | tf_op jit(solution)/shard_map/sub | solution.py:54
  10.4 0.0 collective-permute-done.2
  10.4 0.0 collective-permute-done.3
  10.4 0.0 copy-done
  10.5 0.0 collective-permute-done
  10.6 5.5 %collective-permute-done.1 = f32[3,80,256]{2,1,0:T(8,128)S(1)} collective-permute-done((f32[3,80,256]{2,1,0:T(8,128)}, f32[3,80,256]{2,1,0:T(8,128)S(1)}, u32[]{:S(2)}, u32[]{:S(2)}) %collective-permute-start.1) | collective-permute-done | bytes 245792 | tf_op jit(solution)/shard_map/ppermute | solution.py:21
  16.1 0.1 slice_subtract_fusion.2
  16.2 3.6 %multiply_add_fusion.2 = f32[3,80,256]{2,1,0:T(8,128)S(1)} fusion(f32[3,80,256]{2,1,0:T(8,128)S(1)} %copy-done, f32[3,85,256]{2,1,0:T(8,128)S(1)} %slice_subtract_fusion.5, f32[3,80,261]{2,1,0:T(8,128)S(1)} %fusion, f32[8,80,256]{2,1,0:T(8,128)S(1)} %slice_subtract_fusion.2, f32[80]{0:T(128)S(1)} %get-tuple-element.11, f32[80]{0:T(128)S(1)} %get-tuple-element.12, ...), kind=kLoop, calls=%fused_computation.22 | loop fusion | flops 24268800 | bytes 4916484 | tf_op jit(solution)/shard_map/add | solution.py:107
  19.8 1.9 %collective-permute-start.4 = (f32[3,80,256]{2,1,0:T(8,128)S(1)}, f32[3,80,256]{2,1,0:T(8,128)S(1)}, u32[]{:S(2)}, u32[]{:S(2)}) collective-permute-start(f32[3,80,256]{2,1,0:T(8,128)S(1)} %multiply_add_fusion.2), channel_id=1, source_target_pairs={{0,1},{1,2},{2,3},{3,4},{4,5},{5,6},{6,7},{7,8},{8,9},{9,10},{10,1... | collective-permute-start | bytes 737288 | tf_op jit(solution)/shard_map/ppermute | solution.py:19
  21.7 4.3 %collective-permute-start.5 = (f32[3,80,256]{2,1,0:T(8,128)S(1)}, f32[3,80,256]{2,1,0:T(8,128)S(1)}, u32[]{:S(2)}, u32[]{:S(2)}) collective-permute-start(f32[3,80,256]{2,1,0:T(8,128)S(1)} %multiply_add_fusion.2), channel_id=1, source_target_pairs={{1,0},{2,1},{3,2},{4,3},{5,4},{6,5},{7,6},{8,7},{9,8},{10,9},{11,1... | collective-permute-start | bytes 737288 | tf_op jit(solution)/shard_map/ppermute | solution.py:21
  26.0 1.1 %collective-permute-start.6 = (f32[3,3,256]{2,1,0:T(4,128)S(1)}, f32[3,3,256]{2,1,0:T(4,128)S(1)}, u32[]{:S(2)}, u32[]{:S(2)}) collective-permute-start(f32[3,3,256]{2,1,0:T(4,128)S(1)} %get-tuple-element.7), channel_id=1, source_target_pairs={{0,16},{16,0},{1,17},{17,1},{2,18},{18,2},{3,19},{19,3},{4,20},{20... | collective-permute-start | bytes 27656 | tf_op jit(solution)/shard_map/ppermute | solution.py:19
  27.1 0.1 collective-permute-start.7
  27.2 0.3 fusion.1
  27.4 0.5 collective-permute-done.6
  27.9 0.3 collective-permute-done.7
  28.3 1.2 %collective-permute-done.4 = f32[3,80,256]{2,1,0:T(8,128)S(1)} collective-permute-done((f32[3,80,256]{2,1,0:T(8,128)S(1)}, f32[3,80,256]{2,1,0:T(8,128)S(1)}, u32[]{:S(2)}, u32[]{:S(2)}) %collective-permute-start.4) | collective-permute-done | bytes 245792 | tf_op jit(solution)/shard_map/ppermute | solution.py:19
  29.6 5.1 %collective-permute-done.5 = f32[3,80,256]{2,1,0:T(8,128)S(1)} collective-permute-done((f32[3,80,256]{2,1,0:T(8,128)S(1)}, f32[3,80,256]{2,1,0:T(8,128)S(1)}, u32[]{:S(2)}, u32[]{:S(2)}) %collective-permute-start.5) | collective-permute-done | bytes 245792 | tf_op jit(solution)/shard_map/ppermute | solution.py:21
  34.7 0.1 pad_maximum_fusion
  34.8 0.1 slice_subtract_fusion.1
  34.8 3.6 %multiply_add_fusion.1 = f32[3,80,256]{2,1,0:T(8,128)S(1)} fusion(f32[3,80,256]{2,1,0:T(8,128)S(1)} %multiply_add_fusion.2, f32[3,85,256]{2,1,0:T(8,128)S(1)} %slice_subtract_fusion.4, f32[3,80,261]{2,1,0:T(8,128)S(1)} %fusion.1, f32[8,80,256]{2,1,0:T(8,128)S(1)} %slice_subtract_fusion.1, f32[3,80,256]{2,1,0:T(8,128)S(1)} %copy-done, ...), kind=kLoop, calls=%fused_computation.21 | loop fusion | flops 24453120 | bytes 5162244 | tf_op jit(solution)/shard_map/add | solution.py:108
  38.5 1.9 %collective-permute-start.8 = (f32[3,80,256]{2,1,0:T(8,128)S(1)}, f32[3,80,256]{2,1,0:T(8,128)S(1)}, u32[]{:S(2)}, u32[]{:S(2)}) collective-permute-start(f32[3,80,256]{2,1,0:T(8,128)S(1)} %multiply_add_fusion.1), channel_id=1, source_target_pairs={{0,1},{1,2},{2,3},{3,4},{4,5},{5,6},{6,7},{7,8},{8,9},{9,10},{10,1... | collective-permute-start | bytes 737288 | tf_op jit(solution)/shard_map/ppermute | solution.py:19
  40.4 4.3 %collective-permute-start.9 = (f32[3,80,256]{2,1,0:T(8,128)S(1)}, f32[3,80,256]{2,1,0:T(8,128)S(1)}, u32[]{:S(2)}, u32[]{:S(2)}) collective-permute-start(f32[3,80,256]{2,1,0:T(8,128)S(1)} %multiply_add_fusion.1), channel_id=1, source_target_pairs={{1,0},{2,1},{3,2},{4,3},{5,4},{6,5},{7,6},{8,7},{9,8},{10,9},{11,1... | collective-permute-start | bytes 737288 | tf_op jit(solution)/shard_map/ppermute | solution.py:21
  44.7 1.1 %collective-permute-start.10 = (f32[3,3,256]{2,1,0:T(4,128)S(1)}, f32[3,3,256]{2,1,0:T(4,128)S(1)}, u32[]{:S(2)}, u32[]{:S(2)}) collective-permute-start(f32[3,3,256]{2,1,0:T(4,128)S(1)} %get-tuple-element.5), channel_id=1, source_target_pairs={{0,16},{16,0},{1,17},{17,1},{2,18},{18,2},{3,19},{19,3},{4,20},{20... | collective-permute-start | bytes 27656 | tf_op jit(solution)/shard_map/ppermute | solution.py:19
  45.8 0.1 collective-permute-start.11
  45.9 0.3 fusion.2
  46.1 0.5 collective-permute-done.10
  46.6 0.3 collective-permute-done.11
  47.0 1.3 %collective-permute-done.8 = f32[3,80,256]{2,1,0:T(8,128)S(1)} collective-permute-done((f32[3,80,256]{2,1,0:T(8,128)S(1)}, f32[3,80,256]{2,1,0:T(8,128)S(1)}, u32[]{:S(2)}, u32[]{:S(2)}) %collective-permute-start.8) | collective-permute-done | bytes 245792 | tf_op jit(solution)/shard_map/ppermute | solution.py:19
  48.3 6.3 %collective-permute-done.9 = f32[3,80,256]{2,1,0:T(8,128)S(1)} collective-permute-done((f32[3,80,256]{2,1,0:T(8,128)S(1)}, f32[3,80,256]{2,1,0:T(8,128)S(1)}, u32[]{:S(2)}, u32[]{:S(2)}) %collective-permute-start.9) | collective-permute-done | bytes 245792 | tf_op jit(solution)/shard_map/ppermute | solution.py:21
  54.6 0.1 slice_subtract_fusion
  54.7 4.3 %multiply_add_fusion = f32[3,80,256]{2,1,0:T(8,128)} fusion(f32[3,80,256]{2,1,0:T(8,128)S(1)} %multiply_add_fusion.1, f32[3,85,256]{2,1,0:T(8,128)S(1)} %slice_subtract_fusion.3, f32[3,80,261]{2,1,0:T(8,128)S(1)} %fusion.2, f32[8,80,256]{2,1,0:T(8,128)S(1)} %slice_subtract_fusion, f32[3,80,256]{2,1,0:T(8,128)S(1)} %copy-done, f32[80]{0:T(128)S(1)} %get-tuple-element.11, ...), kind=kLoop, calls=%fused_computation.20 | loop fusion | flops 24453120 | bytes 5162244 | tf_op jit(solution)/shard_map/add | solution.py:109
  (14 shorter events, 0.4 us)
Async XLA Ops:
  0.0 10.5 %collective-permute-start = (f32[3,80,256]{2,1,0:T(8,128)}, f32[3,80,256]{2,1,0:T(8,128)S(1)}, u32[]{:S(2)}, u32[]{:S(2)}) collective-permute-start(f32[3,80,256]{2,1,0:T(8,128)} %param.2), channel_id=1, source_target_pairs={{0,1},{1,2},{2,3},{3,4},{4,5},{5,6},{6,7},{7,8},{8,9},{9,10},{10,1... | collective-permute-start | bytes 737288 | tf_op jit(solution)/shard_map/ppermute | solution.py:19
  3.1 13.0 %collective-permute-start.1 = (f32[3,80,256]{2,1,0:T(8,128)}, f32[3,80,256]{2,1,0:T(8,128)S(1)}, u32[]{:S(2)}, u32[]{:S(2)}) collective-permute-start(f32[3,80,256]{2,1,0:T(8,128)} %param.2), channel_id=1, source_target_pairs={{1,0},{2,1},{3,2},{4,3},{5,4},{6,5},{7,6},{8,7},{9,8},{10,9},{11,1... | collective-permute-start | bytes 737288 | tf_op jit(solution)/shard_map/ppermute | solution.py:21
  7.0 3.4 %collective-permute-start.2 = (f32[3,3,256]{2,1,0:T(4,128)S(1)}, f32[3,3,256]{2,1,0:T(4,128)S(1)}, u32[]{:S(2)}, u32[]{:S(2)}) collective-permute-start(f32[3,3,256]{2,1,0:T(4,128)S(1)} %get-tuple-element.9), channel_id=1, source_target_pairs={{0,16},{16,0},{1,17},{17,1},{2,18},{18,2},{3,19},{19,3},{4,20},{20... | collective-permute-start | bytes 27656 | tf_op jit(solution)/shard_map/ppermute | solution.py:19
  8.2 2.2 %collective-permute-start.3 = (f32[3,3,256]{2,1,0:T(4,128)S(1)}, f32[3,3,256]{2,1,0:T(4,128)S(1)}, u32[]{:S(2)}, u32[]{:S(2)}) collective-permute-start(f32[3,3,256]{2,1,0:T(4,128)S(1)} %get-tuple-element.10), channel_id=1, source_target_pairs={{16,0},{0,16},{17,1},{1,17},{18,2},{2,18},{19,3},{3,19},{20,4},{4,... | collective-permute-start | bytes 27656 | tf_op jit(solution)/shard_map/ppermute | solution.py:21
  8.3 2.1 %copy-start = (f32[3,80,256]{2,1,0:T(8,128)S(1)}, f32[3,80,256]{2,1,0:T(8,128)}, u32[]{:S(2)}) copy-start(f32[3,80,256]{2,1,0:T(8,128)} %param.2) | copy-start | bytes 737284
  19.8 9.8 %collective-permute-start.4 = (f32[3,80,256]{2,1,0:T(8,128)S(1)}, f32[3,80,256]{2,1,0:T(8,128)S(1)}, u32[]{:S(2)}, u32[]{:S(2)}) collective-permute-start(f32[3,80,256]{2,1,0:T(8,128)S(1)} %multiply_add_fusion.2), channel_id=1, source_target_pairs={{0,1},{1,2},{2,3},{3,4},{4,5},{5,6},{6,7},{7,8},{8,9},{9,10},{10,1... | collective-permute-start | bytes 737288 | tf_op jit(solution)/shard_map/ppermute | solution.py:19
  21.7 13.0 %collective-permute-start.5 = (f32[3,80,256]{2,1,0:T(8,128)S(1)}, f32[3,80,256]{2,1,0:T(8,128)S(1)}, u32[]{:S(2)}, u32[]{:S(2)}) collective-permute-start(f32[3,80,256]{2,1,0:T(8,128)S(1)} %multiply_add_fusion.2), channel_id=1, source_target_pairs={{1,0},{2,1},{3,2},{4,3},{5,4},{6,5},{7,6},{8,7},{9,8},{10,9},{11,1... | collective-permute-start | bytes 737288 | tf_op jit(solution)/shard_map/ppermute | solution.py:21
  26.0 2.0 %collective-permute-start.6 = (f32[3,3,256]{2,1,0:T(4,128)S(1)}, f32[3,3,256]{2,1,0:T(4,128)S(1)}, u32[]{:S(2)}, u32[]{:S(2)}) collective-permute-start(f32[3,3,256]{2,1,0:T(4,128)S(1)} %get-tuple-element.7), channel_id=1, source_target_pairs={{0,16},{16,0},{1,17},{17,1},{2,18},{18,2},{3,19},{19,3},{4,20},{20... | collective-permute-start | bytes 27656 | tf_op jit(solution)/shard_map/ppermute | solution.py:19
  27.1 1.2 %collective-permute-start.7 = (f32[3,3,256]{2,1,0:T(4,128)S(1)}, f32[3,3,256]{2,1,0:T(4,128)S(1)}, u32[]{:S(2)}, u32[]{:S(2)}) collective-permute-start(f32[3,3,256]{2,1,0:T(4,128)S(1)} %get-tuple-element.8), channel_id=1, source_target_pairs={{16,0},{0,16},{17,1},{1,17},{18,2},{2,18},{19,3},{3,19},{20,4},{4,... | collective-permute-start | bytes 27656 | tf_op jit(solution)/shard_map/ppermute | solution.py:21
  38.5 9.8 %collective-permute-start.8 = (f32[3,80,256]{2,1,0:T(8,128)S(1)}, f32[3,80,256]{2,1,0:T(8,128)S(1)}, u32[]{:S(2)}, u32[]{:S(2)}) collective-permute-start(f32[3,80,256]{2,1,0:T(8,128)S(1)} %multiply_add_fusion.1), channel_id=1, source_target_pairs={{0,1},{1,2},{2,3},{3,4},{4,5},{5,6},{6,7},{7,8},{8,9},{9,10},{10,1... | collective-permute-start | bytes 737288 | tf_op jit(solution)/shard_map/ppermute | solution.py:19
  40.4 14.2 %collective-permute-start.9 = (f32[3,80,256]{2,1,0:T(8,128)S(1)}, f32[3,80,256]{2,1,0:T(8,128)S(1)}, u32[]{:S(2)}, u32[]{:S(2)}) collective-permute-start(f32[3,80,256]{2,1,0:T(8,128)S(1)} %multiply_add_fusion.1), channel_id=1, source_target_pairs={{1,0},{2,1},{3,2},{4,3},{5,4},{6,5},{7,6},{8,7},{9,8},{10,9},{11,1... | collective-permute-start | bytes 737288 | tf_op jit(solution)/shard_map/ppermute | solution.py:21
  44.7 1.9 %collective-permute-start.10 = (f32[3,3,256]{2,1,0:T(4,128)S(1)}, f32[3,3,256]{2,1,0:T(4,128)S(1)}, u32[]{:S(2)}, u32[]{:S(2)}) collective-permute-start(f32[3,3,256]{2,1,0:T(4,128)S(1)} %get-tuple-element.5), channel_id=1, source_target_pairs={{0,16},{16,0},{1,17},{17,1},{2,18},{18,2},{3,19},{19,3},{4,20},{20... | collective-permute-start | bytes 27656 | tf_op jit(solution)/shard_map/ppermute | solution.py:19
  45.8 1.2 %collective-permute-start.11 = (f32[3,3,256]{2,1,0:T(4,128)S(1)}, f32[3,3,256]{2,1,0:T(4,128)S(1)}, u32[]{:S(2)}, u32[]{:S(2)}) collective-permute-start(f32[3,3,256]{2,1,0:T(4,128)S(1)} %get-tuple-element.6), channel_id=1, source_target_pairs={{16,0},{0,16},{17,1},{1,17},{18,2},{2,18},{19,3},{3,19},{20,4},{4,... | collective-permute-start | bytes 27656 | tf_op jit(solution)/shard_map/ppermute | solution.py:21
where the time goes:
time: 59.2 us; the launch traced here: 58.9 us
  starting transfers between devices  22.2 us (38%)
  waiting for transfers between devices  21.1 us (36%)
  other arithmetic  13.9 us (23%)
  between operations  0.89 us (2%)
  local copies, waits for them, and re-layouts  0.86 us (1%)
    ppermute x6, waiting for transfers between devices, extended_2(): lax.ppermute(head, axis, [((i + 1) % count, i) for i in range(ends)])  17.6 us
    ppermute x6, starting transfers between devices, extended_2(): lax.ppermute(head, axis, [((i + 1) % count, i) for i in range(ends)])  11.8 us
    ppermute x6, starting transfers between devices, extended_2(): lax.ppermute(tail, axis, [(i, (i + 1) % count) for i in range(ends)])  10.4 us
    add x1, other arithmetic, on_device(): level_set / 3.0  4.25 us
    add x1, other arithmetic, on_device(): 0.75 * level_set  3.63 us
    add x1, other arithmetic, on_device(): section_one = level_set + step_size * section_rate(level_set)  3.59 us
    ppermute x6, waiting for transfers between devices, extended_2(): lax.ppermute(tail, axis, [(i, (i + 1) % count) for i in range(ends)])  3.49 us
    sub x9, other arithmetic, one_sided(): lax.slice_in_dim(padded, 1, count + 6, axis=axis)  2.11 us
  transfers between devices with their start and end apart: 12, of which 9 were waited for; matrix products, arithmetic and copies ran while one was open for 5% of the time, Pallas kernels for 0%

commit v1 on v0

v1 whole, which is shorter than its diff:
```python
import functools

import jax
import jax.numpy as jnp
import numpy as np
from jax import lax
from jax.experimental import pallas as pl
from jax.experimental.pallas import tpu as pltpu
from jax.sharding import PartitionSpec as P

MESH = pl.DeviceIdType.MESH
GROUP = 4
GHOST = 3
TILE = 8
LANES = 128
EPSILON = 4.0e-6 / 36.0
SMOOTH = 13.0 / 3.0


def quotient(top, bottom):
    return top / bottom


def indicator(slope, bend):
    whole = slope * slope + bend
    return whole * whole


def bent(second):
    return SMOOTH * (second * second) + EPSILON


def blend_both(d, ga, gb, gc, gd):
    sa, sb, sc = gb - ga, gc - gb, gd - gc
    m = gb + gc
    a = indicator(3.0 * gb - ga, bent(sa))
    b = indicator(m, bent(sb))
    c = indicator(3.0 * gc - gd, bent(sc))
    p, q, r = b * c, 6.0 * (a * c), a * b
    pt, rt = p * (sb - sa), r * (sc - sb)
    two = 2.0 * (pt + rt)
    left = d + m + gc - quotient(two + rt, p + q + 3.0 * r)
    right = d - m - gb + quotient(two + pt, 3.0 * p + q + r)
    return left, right


def differences(values):
    return [after - before for before, after in zip(values, values[1:])]


def sixths(values):
    return [(after - before) * (1.0 / 6.0) for before, after in zip(values, values[1:])]


def interface(u):
    d = differences(u)
    return blend_both(d[2], *sixths(d))


def kernel(sizes, step_ref, level_ref, trig_ref, out_ref, u_zero, u_one, u_two, last, in_send, in_recv, h_send, h_recv, x_send, x_recv, out_send, out_recv):
    block, rows, window, total_gx, total_ha = sizes
    layers = GROUP * block
    gx, ha = lax.axis_index("gx"), lax.axis_index("ha")
    team, pos = ha // GROUP, ha % GROUP

    def gray(n):
        return n + (n // 2) * (5 - 2 * n)

    def window_of(position):
        n = gray(position)
        return n + (gx % 2) * (GROUP - 1 - 2 * n)

    def position_of(number, core):
        return gray(number + (core % 2) * (GROUP - 1 - 2 * number))

    tiles, per = rows // TILE, window // TILE
    extra = tiles - GROUP * (per - 1)

    def start_of(number):
        after = (number + 1) * (per - 1) + jnp.minimum(number + 1, extra)
        return (after - per) * TILE

    w = window_of(pos)
    start = start_of(w)
    peers = [(pos + j) % GROUP for j in range(1, GROUP)]
    peer_ids = [(gx, team * GROUP + p) for p in peers]
    above_gx = (gx + (w + 1) // GROUP) % total_gx
    above_w = (w + 1) % GROUP
    above = (above_gx, team * GROUP + position_of(above_w, above_gx))
    below_gx = (gx + total_gx - (GROUP - w) // GROUP) % total_gx
    below_w = (w + GROUP - 1) % GROUP
    below = (below_gx, team * GROUP + position_of(below_w, below_gx))
    next_team, prior_team = (gx, ha + GROUP), (gx, ha - GROUP)
    has_next, has_prior = team < total_ha // GROUP - 1, team > 0

    rise = jnp.where(w == GROUP - 1, rows - start, start_of(above_w) - start)
    fall = jnp.where(w == 0, 0, start_of(below_w) + window - start)
    rise_row = pl.multiple_of(TILE + rise - TILE, TILE)
    fall_row = pl.multiple_of(TILE + fall, TILE)

    barrier = pltpu.get_barrier_semaphore()
    for device in peer_ids + [above, below]:
        pl.semaphore_signal(barrier, inc=1, device_id=device, device_id_type=MESH)

    @pl.when(has_next)
    def _():
        pl.semaphore_signal(barrier, inc=1, device_id=next_team, device_id_type=MESH)

    @pl.when(has_prior)
    def _():
        pl.semaphore_signal(barrier, inc=1, device_id=prior_team, device_id_type=MESH)

    @pl.when(jnp.logical_not(has_next))
    def _():
        for u in (u_zero, u_one, u_two):
            u[GHOST + layers :] = jnp.zeros((GHOST,) + u.shape[1:], jnp.float32)

    @pl.when(jnp.logical_not(has_prior))
    def _():
        for u in (u_zero, u_one, u_two):
            u[:GHOST] = jnp.zeros((GHOST,) + u.shape[1:], jnp.float32)

    own = pl.multiple_of(start, TILE)
    u_zero[pl.ds(GHOST + block * pos, block), TILE : TILE + window] = level_ref[:, pl.ds(own, window)]

    pl.semaphore_wait(barrier, GROUP + 1 + has_next.astype(jnp.int32) + has_prior.astype(jnp.int32))

    enter = []
    for j in range(GROUP - 1):
        there = pl.multiple_of(start_of(window_of(peers[j])), TILE)
        copy = pltpu.make_async_remote_copy(
            src_ref=level_ref.at[:, pl.ds(there, window)],
            dst_ref=u_zero.at[pl.ds(GHOST + block * pos, block), pl.ds(TILE, window)],
            send_sem=in_send.at[j],
            recv_sem=in_recv.at[j],
            device_id=peer_ids[j],
            device_id_type=MESH,
        )
        copy.start()
        enter.append(copy)
    for copy in enter:
        copy.wait_recv()

    spans = [(0, GHOST), (layers - GHOST, GHOST), (GHOST, layers - 2 * GHOST)]

    def heading_copies(stage, u, span):
        first, count = spans[span]
        where = pl.ds(GHOST + first, count)
        return [
            pltpu.make_async_remote_copy(
                src_ref=u.at[where, pl.ds(source, TILE)],
                dst_ref=u.at[where, pl.ds(target, TILE)],
                send_sem=h_send.at[stage, span, side],
                recv_sem=h_recv.at[stage, span, side],
                device_id=device,
                device_id_type=MESH,
            )
            for side, (source, target, device) in enumerate(
                [(rise_row, 0, above), (fall_row, TILE + window, below)]
            )
        ]

    def layer_copy(stage, u, side):
        source, target, device = [(GHOST, GHOST + layers, prior_team), (layers, 0, next_team)][side]
        return pltpu.make_async_remote_copy(
            src_ref=u.at[pl.ds(source, GHOST), pl.ds(TILE, window)],
            dst_ref=u.at[pl.ds(target, GHOST), pl.ds(TILE, window)],
            send_sem=x_send.at[stage, side],
            recv_sem=x_recv.at[stage, side],
            device_id=device,
            device_id_type=MESH,
        )

    def send_span(stage, u, span):
        if span == 0:
            pl.when(has_prior)(lambda: layer_copy(stage, u, 0).start())
        if span == 1:
            pl.when(has_next)(lambda: layer_copy(stage, u, 1).start())
        for copy in heading_copies(stage, u, span):
            copy.start()

    def await_span(stage, u, span):
        if span == 0:
            pl.when(has_prior)(lambda: layer_copy(stage, u, 1).wait_recv())
        if span == 1:
            pl.when(has_next)(lambda: layer_copy(stage, u, 0).wait_recv())
        for copy in heading_copies(stage, u, span):
            copy.wait_recv()

    lane = lax.broadcasted_iota(jnp.int32, (TILE, LANES), 1)
    halves = out_ref.shape[2] // LANES
    step_size = step_ref[0]
    turn = gx * rows + start

    def shifted(parts, by):
        turned = [pltpu.roll(part, (-by) % LANES, 1) for part in parts]
        if by < 0:
            return [jnp.where(lane < -by, before, here) for before, here in zip([0.0] + turned[:-1], turned)]
        return [jnp.where(lane >= LANES - by, after, here) for here, after in zip(turned, turned[1:] + [0.0])]

    def update(stage, u, target, span):
        first, count = spans[span]

        def tile_step(t, carry):
            row = pl.multiple_of(TILE + t * TILE, TILE)

            near = u.at[:, pl.ds(pl.multiple_of(t * TILE, TILE), 3 * TILE)]

            def cell(layer, half, off=0):
                return near[GHOST + layer, TILE + off : 2 * TILE + off, half * LANES : (half + 1) * LANES]

            cos_half = trig_ref[0, pl.ds(pl.multiple_of(turn + t * TILE, TILE), TILE)]
            sin_half = trig_ref[1, pl.ds(pl.multiple_of(turn + t * TILE, TILE), TILE)]

            ends = [jnp.zeros((TILE, LANES), jnp.float32) for _ in range(GHOST)]
            for n in range(count):
                tail = cell(first + n, halves - 1)
                for back in range(GHOST):
                    moved = pltpu.roll(tail, (GHOST - back + n) % LANES, 1)
                    ends[back] = jnp.where(lane == n, moved, ends[back])
            zero = jnp.zeros((TILE, LANES), jnp.float32)
            _, past = interface(ends + [zero] * 3)

            chain = []
            for half in range(halves):
                x_u = [cell(first + n, half) for n in range(-GHOST, count + GHOST)]
                x_d = differences(x_u)
                x_g = sixths(x_d)
                chain.append((x_d, x_g))
            left_x = [None] * halves
            for half in range(halves):
                x_d, x_g = chain[half]
                left_x[half], _ = blend_both(x_d[2], *x_g[0:4])
            for n in range(count):
                layer = first + n
                here = [cell(layer, half) for half in range(halves)]
                moved = {by: here if by == 0 else shifted(here, by) for by in range(-3, 3)}
                y_left, y_right = [], []
                for half in range(halves):
                    one, two = interface([moved[by][half] for by in range(-3, 3)])
                    y_left.append(one)
                    y_right.append(two)
                turned = [pltpu.roll(part, LANES - 1, 1) for part in y_right]
                turned.append(pltpu.roll(past, (LANES - 1 - n) % LANES, 1))
                y_right = [jnp.where(lane == LANES - 1, turned[i + 1], turned[i]) for i in range(halves)]
                for half in range(halves):
                    x_d, x_g = chain[half]
                    minus_x = left_x[half]
                    left_x[half], plus_x = blend_both(x_d[n + 3], *x_g[n + 1 : n + 5])
                    h_u = [here[half] if off == 0 else cell(layer, half, off) for off in range(-3, 4)]
                    minus_h, _ = interface(h_u[:6])
                    _, plus_h = interface(h_u[1:])
                    minus_y, plus_y = y_left[half], y_right[half]
                    hamilton = (
                        cos_half * (minus_x + plus_x) + sin_half * (minus_y + plus_y)
                    ) - 0.5 * jnp.abs(minus_h + plus_h)
                    rate = (
                        jnp.abs(cos_half) * (plus_x - minus_x)
                        + jnp.abs(sin_half) * (plus_y - minus_y)
                        + 0.5 * (plus_h - minus_h)
                        + jnp.minimum(hamilton, 0.0)
                    )
                    columns = slice(half * LANES, (half + 1) * LANES)
                    moved_on = here[half] + step_size * rate
                    if stage == 0:
                        u_one[GHOST + layer, pl.ds(row, TILE), columns] = moved_on
                    elif stage == 1:
                        base = u_zero[GHOST + layer, pl.ds(row, TILE), columns]
                        u_two[GHOST + layer, pl.ds(row, TILE), columns] = 0.75 * base + 0.25 * moved_on
                    else:
                        base = u_zero[GHOST + layer, pl.ds(row, TILE), columns]
                        last[layer, pl.ds(pl.multiple_of(t * TILE, TILE), TILE), columns] = (
                            base * (1.0 / 3.0) + (2.0 / 3.0) * moved_on
                        )
            return carry

        lax.fori_loop(0, per, tile_step, 0)

    def leave_copy(layer_pos, device, piece, slot):
        first, count = [(TILE, window - TILE), (0, TILE)][piece]
        return pltpu.make_async_remote_copy(
            src_ref=last.at[pl.ds(block * layer_pos, block), pl.ds(first, count)],
            dst_ref=out_ref.at[:, pl.ds(pl.multiple_of(start + first, TILE), count)],
            send_sem=out_send.at[piece, slot],
            recv_sem=out_recv.at[piece, slot],
            device_id=device,
            device_id_type=MESH,
        )

    fields = [u_zero, u_one, u_two]
    for span in range(3):
        send_span(0, u_zero, span)
    for stage in range(3):
        for span in range(3):
            await_span(stage, fields[stage], span)
            update(stage, fields[stage], None, span)
            if stage < 2:
                send_span(stage + 1, fields[stage + 1], span)

    whole = w < extra
    for j in range(GROUP - 1):
        leave_copy(peers[j], peer_ids[j], 0, j).start()
        pl.when(whole)(lambda: leave_copy(peers[j], peer_ids[j], 1, j).start())
    own_late = pl.multiple_of(start + TILE, TILE)
    out_ref[:, pl.ds(own_late, window - TILE)] = last[pl.ds(block * pos, block), TILE:]

    @pl.when(whole)
    def _():
        out_ref[:, pl.ds(own, TILE)] = last[pl.ds(block * pos, block), :TILE]

    for j in range(GROUP - 1):
        from_w = window_of((pos + GROUP - 1 - j) % GROUP)
        leave_copy(peers[j], peer_ids[j], 0, j).wait_recv()
        pl.when(from_w < extra)(lambda: leave_copy(peers[j], peer_ids[j], 1, j).wait_recv())
    for copy in enter:
        copy.wait_send()
    for stage in range(3):
        for span in range(3):
            for copy in heading_copies(stage, fields[stage], span):
                copy.wait_send()
        pl.when(has_prior)(lambda: layer_copy(stage, fields[stage], 0).wait_send())
        pl.when(has_next)(lambda: layer_copy(stage, fields[stage], 1).wait_send())
    for j in range(GROUP - 1):
        leave_copy(peers[j], peer_ids[j], 0, j).wait_send()
        pl.when(whole)(lambda: leave_copy(peers[j], peer_ids[j], 1, j).wait_send())


def on_device(level_set, step_length):
    block, rows, columns = level_set.shape
    total_gx, total_ha = lax.axis_size("gx"), lax.axis_size("ha")
    window = -(-(rows // TILE) // GROUP) * TILE
    angles = 2.0 * np.pi * np.arange(total_gx * rows) / (total_gx * rows)
    trig = np.stack([np.cos(angles), np.sin(angles)]) * 0.5
    trig = jnp.asarray(np.broadcast_to(trig[:, :, None], trig.shape + (LANES,)).astype(np.float32))
    field = pltpu.VMEM((GROUP * block + 2 * GHOST, window + 2 * TILE, columns), jnp.float32)
    dma = pltpu.SemaphoreType.DMA
    cells = block * rows * columns
    return pl.pallas_call(
        functools.partial(kernel, (block, rows, window, total_gx, total_ha)),
        out_shape=jax.ShapeDtypeStruct(level_set.shape, jnp.float32),
        in_specs=[
            pl.BlockSpec(memory_space=pltpu.SMEM),
            pl.BlockSpec(memory_space=pltpu.VMEM),
            pl.BlockSpec(memory_space=pltpu.VMEM),
        ],
        out_specs=pl.BlockSpec(memory_space=pltpu.VMEM),
        scratch_shapes=[
            field,
            field,
            field,
            pltpu.VMEM((GROUP * block, window, columns), jnp.float32),
            dma((GROUP - 1,)),
            dma((GROUP - 1,)),
            dma((3, 3, 2)),
            dma((3, 3, 2)),
            dma((3, 2)),
            dma((3, 2)),
            dma((2, GROUP - 1)),
            dma((2, GROUP - 1)),
        ],
        compiler_params=pltpu.CompilerParams(
            collective_id=0, has_side_effects=True, vmem_limit_bytes=32 * 1024 * 1024
        ),
        cost_estimate=pl.CostEstimate(flops=900 * cells, bytes_accessed=8 * cells, transcendentals=0),
    )(step_length, level_set, trig)


def solution(mesh):
    return jax.shard_map(
        on_device,
        mesh=mesh,
        in_specs=(P("ha", "gx", None), P()),
        out_specs=P("ha", "gx", None),
        check_vma=False,
    )
```

time: 59.2 us -> 35.8 us (0.60)
  the two profiles are of different devices: /device:TPU:29 before, /device:TPU:0 now
where the time goes in v1:
time: 35.8 us; the launch traced here: 35.6 us
  Pallas kernels  32.4 us (91%)
  local copies, waits for them, and re-layouts  2.55 us (7%)
  between operations  0.67 us (2%)
    pallas_call x1, Pallas kernels, on_device(): pl.pallas_call(functools.partial(kernel, (block, rows, window, total_gx,...  32.4 us
    unnamed x5, local copies, waits for them, and re-layouts  2.55 us

profile of v1, /device:TPU:0, one launch (start us, length us, event | category | flops | bytes accessed | tf_op | source)
XLA Modules:
  0.0 35.6 jit_solution(13910926279809346875)
XLA Ops:
  0.7 0.0 copy-start
  0.7 0.9 %copy-done = f32[3,80,256]{2,1,0:T(8,128)S(1)} copy-done((f32[3,80,256]{2,1,0:T(8,128)S(1)}, f32[3,80,256]{2,1,0:T(8,128)}, u32[]{:S(2)}) %copy-start) | copy-done | bytes 245784
  1.6 0.0 copy-start.1
  1.6 0.9 %copy-done.1 = f32[2,160,128]{2,1,0:T(8,128)S(1)} copy-done((f32[2,160,128]{2,1,0:T(8,128)S(1)}, f32[2,160,128]{2,1,0:T(8,128)}, u32[]{:S(2)}) %copy-start.1) | copy-done | bytes 163864
  2.5 32.4 %shard_map.37 = f32[3,80,256]{2,1,0:T(8,128)S(1)} custom-call(f32[1]{0:T(128)S(6)} %copy.5.step_ref, f32[3,80,256]{2,1,0:T(8,128)S(1)} %copy-done, f32[2,160,128]{2,1,0:T(8,128)S(1)} %copy-done.1), custom_call_target="tpu_custom_call" | custom-call | flops 55296000 | bytes 491520 | tf_op jit(solution)/shard_map/pallas_call | solution.py:338
  34.9 0.7 %copy.6 = f32[3,80,256]{2,1,0:T(8,128)} copy(f32[3,80,256]{2,1,0:T(8,128)S(1)} %shard_map.37) | data formatting | bytes 491520
Async XLA Ops:
  0.7 0.9 %copy-start = (f32[3,80,256]{2,1,0:T(8,128)S(1)}, f32[3,80,256]{2,1,0:T(8,128)}, u32[]{:S(2)}) copy-start(f32[3,80,256]{2,1,0:T(8,128)} %level_ref.1) | copy-start | bytes 737284
  1.6 0.9 %copy-start.1 = (f32[2,160,128]{2,1,0:T(8,128)S(1)}, f32[2,160,128]{2,1,0:T(8,128)}, u32[]{:S(2)}) copy-start(f32[2,160,128]{2,1,0:T(8,128)} %constant.2.clone.trig_ref) | copy-start | bytes 491524

commit v2 on v1

--- a/solution.py
+++ b/solution.py
@@ -57,7 +57,7 @@
     return blend_both(d[2], *sixths(d))
 
 
-def kernel(sizes, step_ref, level_ref, trig_ref, out_ref, u_zero, u_one, u_two, last, in_send, in_recv, h_send, h_recv, x_send, x_recv, out_send, out_recv):
+def kernel(sizes, step_ref, level_ref, trig_all, out_ref, u_zero, u_one, u_two, last, trig_ref, own_sem, in_send, in_recv, h_send, h_recv, x_send, x_recv, out_send, out_recv):
     block, rows, window, total_gx, total_ha = sizes
     layers = GROUP * block
     gx, ha = lax.axis_index("gx"), lax.axis_index("ha")
@@ -121,8 +121,15 @@
             u[:GHOST] = jnp.zeros((GHOST,) + u.shape[1:], jnp.float32)
 
     own = pl.multiple_of(start, TILE)
-    u_zero[pl.ds(GHOST + block * pos, block), TILE : TILE + window] = level_ref[:, pl.ds(own, window)]
-
+    turn = pl.multiple_of(gx * rows + start, TILE)
+    own_copy = pltpu.make_async_copy(
+        level_ref.at[:, pl.ds(own, window)],
+        u_zero.at[pl.ds(GHOST + block * pos, block), pl.ds(TILE, window)],
+        own_sem.at[0],
+    )
+    own_copy.start()
+    trig_copy = pltpu.make_async_copy(trig_all.at[:, pl.ds(turn, window)], trig_ref, own_sem.at[1])
+    trig_copy.start()
     pl.semaphore_wait(barrier, GROUP + 1 + has_next.astype(jnp.int32) + has_prior.astype(jnp.int32))
 
     enter = []
@@ -138,14 +145,9 @@
         )
         copy.start()
         enter.append(copy)
-    for copy in enter:
-        copy.wait_recv()
-
-    spans = [(0, GHOST), (layers - GHOST, GHOST), (GHOST, layers - 2 * GHOST)]
 
     def heading_copies(stage, u, span):
-        first, count = spans[span]
-        where = pl.ds(GHOST + first, count)
+        where = pl.ds(GHOST + block * span, block)
         return [
             pltpu.make_async_remote_copy(
                 src_ref=u.at[where, pl.ds(source, TILE)],
@@ -172,17 +174,15 @@
         )
 
     def send_span(stage, u, span):
-        if span == 0:
-            pl.when(has_prior)(lambda: layer_copy(stage, u, 0).start())
-        if span == 1:
-            pl.when(has_next)(lambda: layer_copy(stage, u, 1).start())
+        pl.when((span == 0) & has_prior)(lambda: layer_copy(stage, u, 0).start())
+        pl.when((span == GROUP - 1) & has_next)(lambda: layer_copy(stage, u, 1).start())
         for copy in heading_copies(stage, u, span):
             copy.start()
 
     def await_span(stage, u, span):
         if span == 0:
             pl.when(has_prior)(lambda: layer_copy(stage, u, 1).wait_recv())
-        if span == 1:
+        if span == GROUP - 1:
             pl.when(has_next)(lambda: layer_copy(stage, u, 0).wait_recv())
         for copy in heading_copies(stage, u, span):
             copy.wait_recv()
@@ -190,7 +190,6 @@
     lane = lax.broadcasted_iota(jnp.int32, (TILE, LANES), 1)
     halves = out_ref.shape[2] // LANES
     step_size = step_ref[0]
-    turn = gx * rows + start
 
     def shifted(parts, by):
         turned = [pltpu.roll(part, (-by) % LANES, 1) for part in parts]
@@ -199,7 +198,7 @@
         return [jnp.where(lane >= LANES - by, after, here) for here, after in zip(turned, turned[1:] + [0.0])]
 
     def update(stage, u, target, span):
-        first, count = spans[span]
+        first, count = block * span, block
 
         def tile_step(t, carry):
             row = pl.multiple_of(TILE + t * TILE, TILE)
@@ -209,8 +208,8 @@
             def cell(layer, half, off=0):
                 return near[GHOST + layer, TILE + off : 2 * TILE + off, half * LANES : (half + 1) * LANES]
 
-            cos_half = trig_ref[0, pl.ds(pl.multiple_of(turn + t * TILE, TILE), TILE)]
-            sin_half = trig_ref[1, pl.ds(pl.multiple_of(turn + t * TILE, TILE), TILE)]
+            cos_half = trig_ref[0, pl.ds(pl.multiple_of(t * TILE, TILE), TILE)]
+            sin_half = trig_ref[1, pl.ds(pl.multiple_of(t * TILE, TILE), TILE)]
 
             ends = [jnp.zeros((TILE, LANES), jnp.float32) for _ in range(GHOST)]
             for n in range(count):
@@ -276,53 +275,66 @@
 
         lax.fori_loop(0, per, tile_step, 0)
 
-    def leave_copy(layer_pos, device, piece, slot):
+    def leave_copy(there, piece, sender):
         first, count = [(TILE, window - TILE), (0, TILE)][piece]
         return pltpu.make_async_remote_copy(
-            src_ref=last.at[pl.ds(block * layer_pos, block), pl.ds(first, count)],
+            src_ref=last.at[pl.ds(block * there, block), pl.ds(first, count)],
             dst_ref=out_ref.at[:, pl.ds(pl.multiple_of(start + first, TILE), count)],
-            send_sem=out_send.at[piece, slot],
-            recv_sem=out_recv.at[piece, slot],
-            device_id=device,
+            send_sem=out_send.at[piece, there],
+            recv_sem=out_recv.at[piece, sender],
+            device_id=(gx, team * GROUP + there),
             device_id_type=MESH,
         )
 
+    whole = w < extra
+    own_late = pl.multiple_of(start + TILE, TILE)
+
+    def leave(there):
+        @pl.when(pos != there)
+        def _():
+            leave_copy(there, 0, pos).start()
+            pl.when(whole)(lambda: leave_copy(there, 1, pos).start())
+
+        @pl.when(pos == there)
+        def _():
+            out_ref[:, pl.ds(own_late, window - TILE)] = last[block * there : block * (there + 1), TILE:]
+
+            @pl.when(whole)
+            def _():
+                out_ref[:, pl.ds(own, TILE)] = last[block * there : block * (there + 1), :TILE]
+
     fields = [u_zero, u_one, u_two]
-    for span in range(3):
-        send_span(0, u_zero, span)
+    own_copy.wait()
+    send_span(0, u_zero, pos)
+    for j in range(GROUP - 1):
+        enter[j].wait_recv()
+        send_span(0, u_zero, (pos + GROUP - 1 - j) % GROUP)
+    trig_copy.wait()
+    order = list(range(1, GROUP - 1)) + [0, GROUP - 1]
     for stage in range(3):
-        for span in range(3):
+        for span in order:
             await_span(stage, fields[stage], span)
             update(stage, fields[stage], None, span)
             if stage < 2:
                 send_span(stage + 1, fields[stage + 1], span)
-
-    whole = w < extra
+            else:
+                leave(span)
+
     for j in range(GROUP - 1):
-        leave_copy(peers[j], peer_ids[j], 0, j).start()
-        pl.when(whole)(lambda: leave_copy(peers[j], peer_ids[j], 1, j).start())
-    own_late = pl.multiple_of(start + TILE, TILE)
-    out_ref[:, pl.ds(own_late, window - TILE)] = last[pl.ds(block * pos, block), TILE:]
-
-    @pl.when(whole)
-    def _():
-        out_ref[:, pl.ds(own, TILE)] = last[pl.ds(block * pos, block), :TILE]
-
-    for j in range(GROUP - 1):
-        from_w = window_of((pos + GROUP - 1 - j) % GROUP)
-        leave_copy(peers[j], peer_ids[j], 0, j).wait_recv()
-        pl.when(from_w < extra)(lambda: leave_copy(peers[j], peer_ids[j], 1, j).wait_recv())
+        there = (pos + GROUP - 1 - j) % GROUP
+        leave_copy(there, 0, there).wait_recv()
+        pl.when(window_of(there) < extra)(lambda: leave_copy(there, 1, there).wait_recv())
     for copy in enter:
         copy.wait_send()
     for stage in range(3):
-        for span in range(3):
+        for span in range(GROUP):
             for copy in heading_copies(stage, fields[stage], span):
                 copy.wait_send()
         pl.when(has_prior)(lambda: layer_copy(stage, fields[stage], 0).wait_send())
         pl.when(has_next)(lambda: layer_copy(stage, fields[stage], 1).wait_send())
-    for j in range(GROUP - 1):
-        leave_copy(peers[j], peer_ids[j], 0, j).wait_send()
-        pl.when(whole)(lambda: leave_copy(peers[j], peer_ids[j], 1, j).wait_send())
+    for there in peers:
+        leave_copy(there, 0, pos).wait_send()
+        pl.when(whole)(lambda: leave_copy(there, 1, pos).wait_send())
 
 
 def on_device(level_set, step_length):
@@ -340,8 +352,8 @@
         out_shape=jax.ShapeDtypeStruct(level_set.shape, jnp.float32),
         in_specs=[
             pl.BlockSpec(memory_space=pltpu.SMEM),
-            pl.BlockSpec(memory_space=pltpu.VMEM),
-            pl.BlockSpec(memory_space=pltpu.VMEM),
+            pl.BlockSpec(memory_space=pltpu.HBM),
+            pl.BlockSpec(memory_space=pltpu.HBM),
         ],
         out_specs=pl.BlockSpec(memory_space=pltpu.VMEM),
         scratch_shapes=[
@@ -349,17 +361,19 @@
             field,
             field,
             pltpu.VMEM((GROUP * block, window, columns), jnp.float32),
+            pltpu.VMEM((2, window, LANES), jnp.float32),
+            dma((2,)),
             dma((GROUP - 1,)),
             dma((GROUP - 1,)),
-            dma((3, 3, 2)),
-            dma((3, 3, 2)),
+            dma((3, GROUP, 2)),
+            dma((3, GROUP, 2)),
             dma((3, 2)),
             dma((3, 2)),
-            dma((2, GROUP - 1)),
-            dma((2, GROUP - 1)),
+            dma((2, GROUP)),
+            dma((2, GROUP)),
         ],
         compiler_params=pltpu.CompilerParams(
-            collective_id=0, has_side_effects=True, vmem_limit_bytes=32 * 1024 * 1024
+            collective_id=0, has_side_effects=True, vmem_limit_bytes=63 * 1024 * 1024
         ),
         cost_estimate=pl.CostEstimate(flops=900 * cells, bytes_accessed=8 * cells, transcendentals=0),
     )(step_length, level_set, trig)

time: 35.8 us -> 33.9 us (0.947)
  Pallas kernels: 32.4 us -> 31.4 us
  local copies, waits for them, and re-layouts: 2.55 us -> 1.65 us
    pallas_call x1, Pallas kernels: 32.4 us -> 31.4 us  [on_device(): pl.pallas_call(functools.partial(kernel, (block, rows, window, total_gx,...]
    unnamed x5 -> x1, local copies, waits for them, and re-layouts: 2.55 us -> 1.65 us
where the time goes in v2:
time: 33.9 us; the launch traced here: 33.7 us
  Pallas kernels  31.4 us (93%)
  local copies, waits for them, and re-layouts  1.65 us (5%)
  between operations  0.66 us (2%)
    pallas_call x1, Pallas kernels, on_device(): pl.pallas_call(functools.partial(kernel, (block, rows, window, total_gx,...  31.4 us
    unnamed x1, local copies, waits for them, and re-layouts  1.65 us

profile of v2, /device:TPU:0, one launch (start us, length us, event | category | flops | bytes accessed | tf_op | source)
XLA Modules:
  0.0 33.7 jit_solution(7849873335226340984)
XLA Ops:
  0.7 31.4 %shard_map.37 = f32[3,80,256]{2,1,0:T(8,128)} custom-call(f32[1]{0:T(128)S(6)} %copy.5.step_ref, f32[3,80,256]{2,1,0:T(8,128)} %level_ref.1, f32[2,160,128]{2,1,0:T(8,128)} %constant.2.clone.trig_all), custom_call_target="tpu_custom_call" | custom-call | flops 55296000 | bytes 491520 | tf_op jit(solution)/shard_map/pallas_call | solution.py:350
  32.1 1.7 %copy.6 = f32[3,80,256]{2,1,0:T(8,128)} copy(f32[3,80,256]{2,1,0:T(8,128)} %shard_map.37) | data formatting | bytes 491520

commit v3 on v2

--- a/solution.py
+++ b/solution.py
@@ -57,7 +57,7 @@
     return blend_both(d[2], *sixths(d))
 
 
-def kernel(sizes, step_ref, level_ref, trig_all, out_ref, u_zero, u_one, u_two, last, trig_ref, own_sem, in_send, in_recv, h_send, h_recv, x_send, x_recv, out_send, out_recv):
+def kernel(sizes, step_ref, level_ref, out_ref, u_zero, u_one, u_two, last, trig_ref, own_sem, in_send, in_recv, h_send, h_recv, x_send, x_recv, out_send, out_recv):
     block, rows, window, total_gx, total_ha = sizes
     layers = GROUP * block
     gx, ha = lax.axis_index("gx"), lax.axis_index("ha")
@@ -121,37 +121,45 @@
             u[:GHOST] = jnp.zeros((GHOST,) + u.shape[1:], jnp.float32)
 
     own = pl.multiple_of(start, TILE)
-    turn = pl.multiple_of(gx * rows + start, TILE)
-    own_copy = pltpu.make_async_copy(
-        level_ref.at[:, pl.ds(own, window)],
-        u_zero.at[pl.ds(GHOST + block * pos, block), pl.ds(TILE, window)],
-        own_sem.at[0],
-    )
-    own_copy.start()
-    trig_copy = pltpu.make_async_copy(trig_all.at[:, pl.ds(turn, window)], trig_ref, own_sem.at[1])
-    trig_copy.start()
+    halves = out_ref.shape[2] // LANES
+
+    def block_part(from_row, half):
+        return (
+            level_ref.at[:, pl.ds(from_row, window), pl.ds(half * LANES, LANES)],
+            u_zero.at[pl.ds(GHOST + block * pos, block), half, pl.ds(TILE, window)],
+        )
+
+    own_copies = [pltpu.make_async_copy(*block_part(own, half), own_sem.at[half]) for half in range(halves)]
+    for copy in own_copies:
+        copy.start()
     pl.semaphore_wait(barrier, GROUP + 1 + has_next.astype(jnp.int32) + has_prior.astype(jnp.int32))
 
     enter = []
     for j in range(GROUP - 1):
         there = pl.multiple_of(start_of(window_of(peers[j])), TILE)
-        copy = pltpu.make_async_remote_copy(
-            src_ref=level_ref.at[:, pl.ds(there, window)],
-            dst_ref=u_zero.at[pl.ds(GHOST + block * pos, block), pl.ds(TILE, window)],
-            send_sem=in_send.at[j],
-            recv_sem=in_recv.at[j],
-            device_id=peer_ids[j],
-            device_id_type=MESH,
-        )
-        copy.start()
-        enter.append(copy)
+        for half in range(halves):
+            source, target = block_part(there, half)
+            copy = pltpu.make_async_remote_copy(
+                src_ref=source,
+                dst_ref=target,
+                send_sem=in_send.at[j, half],
+                recv_sem=in_recv.at[j, half],
+                device_id=peer_ids[j],
+                device_id_type=MESH,
+            )
+            copy.start()
+            enter.append(copy)
+    turn_cells = gx * rows + start + lax.broadcasted_iota(jnp.int32, (window, LANES), 0)
+    heading = turn_cells.astype(jnp.float32) * (2.0 * np.pi / (total_gx * rows))
+    trig_ref[0] = 0.5 * jnp.cos(heading)
+    trig_ref[1] = 0.5 * jnp.sin(heading)
 
     def heading_copies(stage, u, span):
         where = pl.ds(GHOST + block * span, block)
         return [
             pltpu.make_async_remote_copy(
-                src_ref=u.at[where, pl.ds(source, TILE)],
-                dst_ref=u.at[where, pl.ds(target, TILE)],
+                src_ref=u.at[where, :, pl.ds(source, TILE)],
+                dst_ref=u.at[where, :, pl.ds(target, TILE)],
                 send_sem=h_send.at[stage, span, side],
                 recv_sem=h_recv.at[stage, span, side],
                 device_id=device,
@@ -165,8 +173,8 @@
     def layer_copy(stage, u, side):
         source, target, device = [(GHOST, GHOST + layers, prior_team), (layers, 0, next_team)][side]
         return pltpu.make_async_remote_copy(
-            src_ref=u.at[pl.ds(source, GHOST), pl.ds(TILE, window)],
-            dst_ref=u.at[pl.ds(target, GHOST), pl.ds(TILE, window)],
+            src_ref=u.at[pl.ds(source, GHOST), :, pl.ds(TILE, window)],
+            dst_ref=u.at[pl.ds(target, GHOST), :, pl.ds(TILE, window)],
             send_sem=x_send.at[stage, side],
             recv_sem=x_recv.at[stage, side],
             device_id=device,
@@ -188,7 +196,6 @@
             copy.wait_recv()
 
     lane = lax.broadcasted_iota(jnp.int32, (TILE, LANES), 1)
-    halves = out_ref.shape[2] // LANES
     step_size = step_ref[0]
 
     def shifted(parts, by):
@@ -203,10 +210,10 @@
         def tile_step(t, carry):
             row = pl.multiple_of(TILE + t * TILE, TILE)
 
-            near = u.at[:, pl.ds(pl.multiple_of(t * TILE, TILE), 3 * TILE)]
+            near = u.at[:, :, pl.ds(pl.multiple_of(t * TILE, TILE), 3 * TILE)]
 
             def cell(layer, half, off=0):
-                return near[GHOST + layer, TILE + off : 2 * TILE + off, half * LANES : (half + 1) * LANES]
+                return near[GHOST + layer, half, TILE + off : 2 * TILE + off]
 
             cos_half = trig_ref[0, pl.ds(pl.multiple_of(t * TILE, TILE), TILE)]
             sin_half = trig_ref[1, pl.ds(pl.multiple_of(t * TILE, TILE), TILE)]
@@ -262,12 +269,12 @@
                     columns = slice(half * LANES, (half + 1) * LANES)
                     moved_on = here[half] + step_size * rate
                     if stage == 0:
-                        u_one[GHOST + layer, pl.ds(row, TILE), columns] = moved_on
+                        u_one[GHOST + layer, half, pl.ds(row, TILE)] = moved_on
                     elif stage == 1:
-                        base = u_zero[GHOST + layer, pl.ds(row, TILE), columns]
-                        u_two[GHOST + layer, pl.ds(row, TILE), columns] = 0.75 * base + 0.25 * moved_on
+                        base = u_zero[GHOST + layer, half, pl.ds(row, TILE)]
+                        u_two[GHOST + layer, half, pl.ds(row, TILE)] = 0.75 * base + 0.25 * moved_on
                     else:
-                        base = u_zero[GHOST + layer, pl.ds(row, TILE), columns]
+                        base = u_zero[GHOST + layer, half, pl.ds(row, TILE)]
                         last[layer, pl.ds(pl.multiple_of(t * TILE, TILE), TILE), columns] = (
                             base * (1.0 / 3.0) + (2.0 / 3.0) * moved_on
                         )
@@ -304,12 +311,13 @@
                 out_ref[:, pl.ds(own, TILE)] = last[block * there : block * (there + 1), :TILE]
 
     fields = [u_zero, u_one, u_two]
-    own_copy.wait()
+    for copy in own_copies:
+        copy.wait()
     send_span(0, u_zero, pos)
     for j in range(GROUP - 1):
-        enter[j].wait_recv()
+        for half in range(halves):
+            enter[j * halves + half].wait_recv()
         send_span(0, u_zero, (pos + GROUP - 1 - j) % GROUP)
-    trig_copy.wait()
     order = list(range(1, GROUP - 1)) + [0, GROUP - 1]
     for stage in range(3):
         for span in order:
@@ -341,10 +349,8 @@
     block, rows, columns = level_set.shape
     total_gx, total_ha = lax.axis_size("gx"), lax.axis_size("ha")
     window = -(-(rows // TILE) // GROUP) * TILE
-    angles = 2.0 * np.pi * np.arange(total_gx * rows) / (total_gx * rows)
-    trig = np.stack([np.cos(angles), np.sin(angles)]) * 0.5
-    trig = jnp.asarray(np.broadcast_to(trig[:, :, None], trig.shape + (LANES,)).astype(np.float32))
-    field = pltpu.VMEM((GROUP * block + 2 * GHOST, window + 2 * TILE, columns), jnp.float32)
+    halves = columns // LANES
+    field = pltpu.VMEM((GROUP * block + 2 * GHOST, halves, window + 2 * TILE, LANES), jnp.float32)
     dma = pltpu.SemaphoreType.DMA
     cells = block * rows * columns
     return pl.pallas_call(
@@ -352,7 +358,6 @@
         out_shape=jax.ShapeDtypeStruct(level_set.shape, jnp.float32),
         in_specs=[
             pl.BlockSpec(memory_space=pltpu.SMEM),
-            pl.BlockSpec(memory_space=pltpu.HBM),
             pl.BlockSpec(memory_space=pltpu.HBM),
         ],
         out_specs=pl.BlockSpec(memory_space=pltpu.VMEM),
@@ -362,9 +367,9 @@
             field,
             pltpu.VMEM((GROUP * block, window, columns), jnp.float32),
             pltpu.VMEM((2, window, LANES), jnp.float32),
-            dma((2,)),
-            dma((GROUP - 1,)),
-            dma((GROUP - 1,)),
+            dma((halves,)),
+            dma((GROUP - 1, halves)),
+            dma((GROUP - 1, halves)),
             dma((3, GROUP, 2)),
             dma((3, GROUP, 2)),
             dma((3, 2)),
@@ -373,10 +378,10 @@
             dma((2, GROUP)),
         ],
         compiler_params=pltpu.CompilerParams(
-            collective_id=0, has_side_effects=True, vmem_limit_bytes=63 * 1024 * 1024
+            collective_id=0, has_side_effects=True, vmem_limit_bytes=32 * 1024 * 1024
         ),
         cost_estimate=pl.CostEstimate(flops=900 * cells, bytes_accessed=8 * cells, transcendentals=0),
-    )(step_length, level_set, trig)
+    )(step_length, level_set)
 
 
 def solution(mesh):

time: 33.9 us -> 29.9 us (0.88)
  Pallas kernels: 31.4 us -> 27.5 us
    pallas_call x1, Pallas kernels: 31.4 us -> 27.5 us  [on_device(): pl.pallas_call(functools.partial(kernel, (block, rows, window, total_gx,...]
    unnamed x1 -> x3, local copies, waits for them, and re-layouts: 1.65 us -> 1.63 us
where the time goes in v3:
time: 29.9 us; the launch traced here: 29.8 us
  Pallas kernels  27.5 us (92%)
  local copies, waits for them, and re-layouts  1.63 us (5%)
  between operations  0.67 us (2%)
    pallas_call x1, Pallas kernels, on_device(): pl.pallas_call(functools.partial(kernel, (block, rows, window, total_gx,...  27.5 us
    unnamed x3, local copies, waits for them, and re-layouts  1.63 us

profile of v3, /device:TPU:0, one launch (start us, length us, event | category | flops | bytes accessed | tf_op | source)
XLA Modules:
  0.0 29.8 jit_solution(13440052294752963329)
XLA Ops:
  0.7 0.0 copy-start
  0.7 0.9 %copy-done = f32[3,80,256]{2,1,0:T(8,128)S(1)} copy-done((f32[3,80,256]{2,1,0:T(8,128)S(1)}, f32[3,80,256]{2,1,0:T(8,128)}, u32[]{:S(2)}) %copy-start) | copy-done | bytes 245784
  1.6 27.5 %shard_map.28 = f32[3,80,256]{2,1,0:T(8,128)S(1)} custom-call(f32[1]{0:T(128)S(6)} %copy.4.step_ref, f32[3,80,256]{2,1,0:T(8,128)S(1)} %copy-done), custom_call_target="tpu_custom_call" | custom-call | flops 55296000 | bytes 491520 | tf_op jit(solution)/shard_map/pallas_call | solution.py:356
  29.1 0.7 %copy.5 = f32[3,80,256]{2,1,0:T(8,128)} copy(f32[3,80,256]{2,1,0:T(8,128)S(1)} %shard_map.28) | data formatting | bytes 491520
Async XLA Ops:
  0.7 0.9 %copy-start = (f32[3,80,256]{2,1,0:T(8,128)S(1)}, f32[3,80,256]{2,1,0:T(8,128)}, u32[]{:S(2)}) copy-start(f32[3,80,256]{2,1,0:T(8,128)} %level_ref.1) | copy-start | bytes 737284

commit v4 on v3

--- a/solution.py
+++ b/solution.py
@@ -280,7 +280,7 @@
                         )
             return carry
 
-        lax.fori_loop(0, per, tile_step, 0)
+        lax.fori_loop(0, per, tile_step, 0, unroll=True)
 
     def leave_copy(there, piece, sender):
         first, count = [(TILE, window - TILE), (0, TILE)][piece]

time: 29.9 us -> 28.7 us (0.960)
  Pallas kernels: 27.5 us -> 26.3 us
    pallas_call x1, Pallas kernels: 27.5 us -> 26.3 us  [on_device(): pl.pallas_call(functools.partial(kernel, (block, rows, window, total_gx,...]
where the time goes in v4:
time: 28.7 us; the launch traced here: 28.6 us
  Pallas kernels  26.3 us (92%)
  local copies, waits for them, and re-layouts  1.63 us (6%)
  between operations  0.67 us (2%)
    pallas_call x1, Pallas kernels, on_device(): pl.pallas_call(functools.partial(kernel, (block, rows, window, total_gx,...  26.3 us
    unnamed x3, local copies, waits for them, and re-layouts  1.63 us

profile of v4, /device:TPU:0, one launch (start us, length us, event | category | flops | bytes accessed | tf_op | source)
XLA Modules:
  0.0 28.6 jit_solution(12078071275654719295)
XLA Ops:
  0.7 0.0 copy-start
  0.7 0.9 %copy-done = f32[3,80,256]{2,1,0:T(8,128)S(1)} copy-done((f32[3,80,256]{2,1,0:T(8,128)S(1)}, f32[3,80,256]{2,1,0:T(8,128)}, u32[]{:S(2)}) %copy-start) | copy-done | bytes 245784
  1.6 26.3 %shard_map.28 = f32[3,80,256]{2,1,0:T(8,128)S(1)} custom-call(f32[1]{0:T(128)S(6)} %copy.4.step_ref, f32[3,80,256]{2,1,0:T(8,128)S(1)} %copy-done), custom_call_target="tpu_custom_call" | custom-call | flops 55296000 | bytes 491520 | tf_op jit(solution)/shard_map/pallas_call | solution.py:356
  27.9 0.7 %copy.5 = f32[3,80,256]{2,1,0:T(8,128)} copy(f32[3,80,256]{2,1,0:T(8,128)S(1)} %shard_map.28) | data formatting | bytes 491520
Async XLA Ops:
  0.7 0.9 %copy-start = (f32[3,80,256]{2,1,0:T(8,128)S(1)}, f32[3,80,256]{2,1,0:T(8,128)}, u32[]{:S(2)}) copy-start(f32[3,80,256]{2,1,0:T(8,128)} %level_ref.1) | copy-start | bytes 737284
